TPU v7x, 32 devices: a whole 2x2x4 slice. The times are simulated.
32 devices in a mesh: space: 8 (over z, y), dp: 4 (over x, core).
Axes of the slice: x: 2, y: 2, z: 4, core: 2. Of those that a mesh axis runs over, the one named last changes fastest.
Arguments:
- forcing: bfloat16 [4, 128, 16, 8, 128], P('dp', 'space'), may hold values from -6 to 6
- hidden_prev: bfloat16 [4, 128, 64, 8, 128], P('dp', 'space'), may hold values from -0.8984375 to 0.8984375
- cell_prev: bfloat16 [4, 128, 64, 8, 128], P('dp', 'space'), may hold values from -4 to 4
- hidden_grad: bfloat16 [4, 128, 64, 8, 128], P('dp', 'space'), may hold values from -0.0625 to 0.0625
- w_gates: bfloat16 [256, 720], replicated, may hold values from -0.21875 to 0.21875
- gate_bias: float32 [256], replicated, may hold values from -4 to 4
- worker: int32 [4, 128], P('dp'), may hold values from -1 to 7, as said below
Outputs:
- hidden_next: bfloat16 [4, 128, 64, 8, 128], P('dp', 'space')
- cell_next: bfloat16 [4, 128, 64, 8, 128], P('dp', 'space')
- weight_grad: float32 [256, 720], P('space')
- bias_grad: float32 [256], P('space')
Inputs may be any that keep to these rules, and one draw needn't show every extreme that they name: Each year's active tiles (worker >= 0) are dealt to workers in increasing tile order: the j-th active tile, from 0, goes to worker j modulo the number of devices along space; every year has exactly 8 active tiles for every worker, one home in every year has all 16 of its tiles active, and so at most 2 tiles, reached, go from one home to one worker.
All inputs are finite; a program needn't handle non-finite values.
Results may differ from a plain program's by a relative error of at most 0.0075.
Values may be sent and summed in bfloat16 or wider, within the bound.
A program may use at most 64 MiB of HBM per device.

v0:
```python
import jax
import jax.numpy as jnp
from jax import lax
from jax.sharding import PartitionSpec as P

TW = 4
BAND = 4


def extended(array, sides, width):
    for axis, dim in sides:
        size, length = (lax.axis_size(axis), array.shape[dim])
        up = [(i, (i + 1) % size) for i in range(size - 1)]
        down = [(j, i) for i, j in up]
        last = lax.slice_in_dim(array, length - width, length, axis=dim)
        leading = lax.slice_in_dim(array, 0, width, axis=dim)
        before = lax.ppermute(last, axis, up)
        after = lax.ppermute(leading, axis, down)
        array = jnp.concatenate([before, array, after], axis=dim)
    return array


def tile_step(window, cell_old, out_grad, flag, w_gates, gate_bias):
    in_width, rows_pad, cols_pad = window.shape
    tile_rows = rows_pad - 2
    tile_cols = cols_pad - 2
    hidden_width = cell_old.shape[0]
    cells = tile_rows * tile_cols
    patches = jnp.concatenate(
        [
            window[:, row_off : row_off + tile_rows, col_off : col_off + tile_cols].reshape(
                in_width, cells
            )
            for row_off in range(3)
            for col_off in range(3)
        ],
        axis=0,
    )
    pre = jnp.dot(w_gates, patches, preferred_element_type=jnp.float32) + gate_bias[:, None]
    pre = pre.reshape(4, hidden_width, cells)
    in_gate = jax.nn.sigmoid(pre[0])
    forget_gate = jax.nn.sigmoid(pre[1])
    out_gate = jax.nn.sigmoid(pre[2])
    candidate = jnp.tanh(pre[3])
    cell_before = cell_old.reshape(hidden_width, cells).astype(jnp.float32)
    cell_full = forget_gate * cell_before + in_gate * candidate
    squashed = jnp.tanh(cell_full)
    hidden_full = out_gate * squashed
    upstream = out_grad.reshape(hidden_width, cells).astype(jnp.float32)
    d_cell = upstream * out_gate * (1.0 - squashed * squashed)
    gate_grad = jnp.concatenate(
        [
            d_cell * candidate * in_gate * (1.0 - in_gate),
            d_cell * cell_before * forget_gate * (1.0 - forget_gate),
            upstream * squashed * out_gate * (1.0 - out_gate),
            d_cell * in_gate * (1.0 - candidate * candidate),
        ],
        axis=0,
    )
    gate_grad = (gate_grad * flag).astype(jnp.bfloat16)
    weight_part = lax.dot_general(
        gate_grad, patches, (((1,), (1,)), ((), ())), preferred_element_type=jnp.float32
    )
    bias_part = jnp.sum(gate_grad.astype(jnp.float32), axis=1)
    hidden_new = hidden_full.astype(jnp.bfloat16).reshape(hidden_width, tile_rows, tile_cols)
    cell_new = cell_full.astype(jnp.bfloat16).reshape(hidden_width, tile_rows, tile_cols)
    return (hidden_new, cell_new, weight_part, bias_part)


def run_tiles(windows, cell_olds, out_grads, flags, w_gates, gate_bias, grad_init):

    def one_tile(carry, item):
        window, cell_old, out_grad, flag = item
        hidden_new, cell_new, weight_part, bias_part = tile_step(
            window, cell_old, out_grad, flag, w_gates, gate_bias
        )
        return ((carry[0] + weight_part, carry[1] + bias_part), (hidden_new, cell_new))

    return lax.scan(one_tile, grad_init, (windows, cell_olds, out_grads, flags))


def shards(forcing, hidden_prev, cell_prev, hidden_grad, w_gates, gate_bias, worker):
    years, tiles_home, in_ch, tile_rows, tile_cols = forcing.shape
    hidden_width = hidden_prev.shape[2]
    in_width = in_ch + hidden_width
    my_index = lax.axis_index("space")
    grad_state = (jnp.zeros(w_gates.shape, jnp.float32), jnp.zeros(gate_bias.shape, jnp.float32))
    whole = worker[0]
    mine = lax.dynamic_slice_in_dim(whole, my_index * tiles_home, tiles_home)
    my_live = mine >= 0
    joined = jnp.concatenate([forcing[0], hidden_prev[0]], axis=1)
    band = joined.reshape(BAND, TW, in_width, tile_rows, tile_cols).transpose(2, 0, 3, 1, 4)
    band = band.reshape(in_width, BAND * tile_rows, TW * tile_cols)
    grown = extended(band, (("space", 1),), 1)
    grown = jnp.pad(grown, ((0, 0), (0, 0), (1, 1)))
    windows = jnp.stack(
        [
            grown[
                :,
                block_row * tile_rows : block_row * tile_rows + tile_rows + 2,
                block_col * tile_cols : block_col * tile_cols + tile_cols + 2,
            ]
            for block_row in range(BAND)
            for block_col in range(TW)
        ]
    )
    flags = my_live.astype(jnp.float32)
    grad_state, (hidden_done, cell_done) = run_tiles(
        windows, cell_prev[0], hidden_grad[0], flags, w_gates, gate_bias, grad_state
    )
    live_mask = my_live[:, None, None, None]
    hidden_list = [jnp.where(live_mask, hidden_done, hidden_prev[0])]
    cell_list = [jnp.where(live_mask, cell_done, cell_prev[0])]
    grad_weights, grad_bias = grad_state
    part_weights, part_bias = (
        lax.psum_scatter(grad_weights, "space", scatter_dimension=0, tiled=True),
        lax.psum_scatter(grad_bias, "space", scatter_dimension=0, tiled=True),
    )
    out_weights, out_bias = lax.psum((part_weights, part_bias), "dp")
    return (jnp.stack(hidden_list), jnp.stack(cell_list), out_weights, out_bias)


def solution(mesh):
    placed = (
        P("dp", "space", None, None, None),
        P("dp", "space", None, None, None),
        P("dp", "space", None, None, None),
        P("dp", "space", None, None, None),
        P(),
        P(),
        P("dp", None),
    )
    return jax.shard_map(
        shards,
        mesh=mesh,
        in_specs=placed,
        out_specs=(
            P("dp", "space", None, None, None),
            P("dp", "space", None, None, None),
            P("space", None),
            P("space"),
        ),
        check_vma=False,
    )
```

profile of v0, /device:TPU:0, one launch (start us, length us, event | category | flops | bytes accessed | tf_op | source)
XLA Modules:
  0.0 275.8 jit_solution(15444297955244776131)
XLA Ops:
  7.2 2.1 copy_bitcast_fusion
  9.5 4.9 %collective-permute-start = (bf16[80,1,512]{2,1,0:T(2,128)(2,1)S(1)}, bf16[80,1,512]{2,1,0:T(2,128)(2,1)S(1)}, u32[]{:S(2)}, u32[]{:S(2)}) collective-permute-start(bf16[80,1,512]{2,1,0:T(2,128)(2,1)S(1)} %get-tuple-element.150), channel_id=1, source_target_pairs={{0,4},{4,8},{8,12},{12,16},{16,20},{20,24},{24,28},{1,5},{5,9},{9,... | collective-permute-start | bytes 245768 | tf_op jit(solution)/shard_map/ppermute | solution.py:17
  15.9 2.0 collective-permute-done
  17.9 4.1 %collective-permute-done.1 = bf16[80,1,512]{2,1,0:T(2,128)(2,1)S(1)} collective-permute-done((bf16[80,1,512]{2,1,0:T(2,128)(2,1)S(1)}, bf16[80,1,512]{2,1,0:T(2,128)(2,1)S(1)}, u32[]{:S(2)}, u32[]{:S(2)}) %collective-permute-start.1) | collective-permute-done | bytes 81952 | tf_op jit(solution)/shard_map/ppermute | solution.py:18
  22.0 4.4 %fusion.30 = bf16[80,34,514]{2,1,0:T(8,128)(2,1)S(1)} fusion(bf16[80,1,512]{2,1,0:T(2,128)(2,1)S(1)} %collective-permute-done.1, bf16[80,32,512]{2,1,0:T(8,128)(2,1)S(1)} %copy_bitcast_fusion, bf16[80,1,512]{2,1,0:T(2,128)(2,1)S(1)} %collective-permute-done), kind=kLoop, calls=%fused_computation.62 | loop fusion | flops 16776960 | bytes 5581440 | tf_op jit(solution)/shard_map/concatenate | solution.py:19
  32.5 4.0 %copy-done.1 = bf16[16,80,10,130]{3,2,1,0:T(8,128)(2,1)} copy-done((bf16[16,80,10,130]{3,2,1,0:T(8,128)(2,1)}, bf16[16,80,10,130]{3,2,1,0:T(8,128)(2,1)S(1)}, u32[]{:S(2)}) %copy-start.1) | copy-done | bytes 3328024
  36.4 133.0 %while.17 = (s32[]{:T(128)}, f32[256,720]{0,1:T(8,128)S(1)}, f32[256]{0:T(256)S(1)}, bf16[16,64,8,128]{3,2,1,0:T(8,128)(2,1)}, bf16[16,64,8,128]{3,2,1,0:T(8,128...) while((s32[]{:T(128)}, f32[256,720]{0,1:T(8,128)S(1)}, ...), condition=%wide.region_2.3_spmd.clone, body=%wide.region_0.2_spmd.clone.sunk | while | flops 762552576 | bytes 26218424 | solution.py:79
  39.6 1.7 convert_dynamic-update-slice_fusion.2
  48.0 1.7 convert_dynamic-update-slice_fusion.2
  51.7 1.3 convolution_add_fusion.3
  56.3 1.7 convert_dynamic-update-slice_fusion.2
  64.6 1.7 convert_dynamic-update-slice_fusion.2
  68.3 1.3 convolution_add_fusion.3
  72.9 1.7 convert_dynamic-update-slice_fusion.2
  81.2 1.7 convert_dynamic-update-slice_fusion.2
  85.0 1.3 convolution_add_fusion.3
  89.5 1.7 convert_dynamic-update-slice_fusion.2
  97.8 1.7 convert_dynamic-update-slice_fusion.2
  106.1 1.7 convert_dynamic-update-slice_fusion.2
  114.4 1.7 convert_dynamic-update-slice_fusion.2
  122.8 1.7 convert_dynamic-update-slice_fusion.2
  131.1 1.7 convert_dynamic-update-slice_fusion.2
  139.4 1.7 convert_dynamic-update-slice_fusion.2
  147.7 1.7 convert_dynamic-update-slice_fusion.2
  156.0 1.7 convert_dynamic-update-slice_fusion.2
  164.3 1.7 convert_dynamic-update-slice_fusion.2
  171.9 62.8 %reduce-scatter.2.cloned.1.call-done = f32[32,720]{1,0:T(8,128)} async-done(((f32[256,720]{1,0:T(8,128)}), f32[32,720]{1,0:T(8,128)}) %reduce-scatter.2.cloned.1.call-update) | async-done | bytes 92176 | tf_op jit(solution)/shard_map/reduce_scatter | solution.py:116
  234.8 5.3 %select_bitcast_fusion = (bf16[1,16,64,8,128]{4,3,2,1,0:T(8,128)(2,1)}, bf16[1,16,64,8,128]{4,3,2,1,0:T(8,128)(2,1)}) fusion(bf16[16,64,8,128]{3,2,1,0:T(8,128)(2,1)} %get-tuple-element.65, pred[16]{0:T(512)(128)(4,1)S(1)} %get-tuple-element.130, bf16[1,16,64,8,128]{4,3,2,1,0:T(8,128)(2,1)} %bitcast.255, bf16[16,64,8,128]{3,2,1,0:T(8,128)(2,1)} %get-tuple-element.64, ...), kind=kLoop, calls=%fused_computation.67 | loop fusion | flops 2097152 | bytes 12582928 | tf_op jit(solution)/shard_map/stack | solution.py:120
  240.1 19.3 %all-reduce.1 = f32[256]{0:T(256)S(1)} all-reduce(f32[256]{0:T(256)S(1)} %get-tuple-element.67), channel_id=3, replica_groups=mesh['space'=8,'dp'=4] {'space'}, use_global_device_ids=true, to_apply=%region_5.6.clone | all-reduce | flops 256 | bytes 2048
  259.5 6.1 %psum.15 = f32[32]{0:T(128)} all-reduce(f32[32]{0:T(128)S(1)} %dynamic-slice.2), channel_id=1, replica_groups=mesh['space'=8,'dp'=4] {'dp'}, use_global_device_ids=true, to_apply=%region_6.7 | all-reduce | flops 32 | bytes 256 | tf_op jit(solution)/shard_map/psum | solution.py:119
  265.6 1.8 all-reduce.4.cloned.1.call-done
  267.5 1.5 copy.115
  (422 shorter events, 108.1 us)
Async XLA Ops:
  7.2 227.6 %reduce-scatter.2.cloned.1.call-start = ((), (), s32[]{:S(2)}) async-start(), calls=%async_computation.1 | async-start | bytes 884736 | tf_op jit(solution)/shard_map/reduce_scatter | solution.py:116
  7.2 8.6 %copy-start.3 = (s32[1,128]{1,0:T(1,128)S(1)}, s32[1,128]{1,0:T(1,128)}, u32[]{:S(2)}) copy-start(s32[1,128]{1,0:T(1,128)} %param.15) | copy-start | bytes 1540
  9.5 8.3 %collective-permute-start = (bf16[80,1,512]{2,1,0:T(2,128)(2,1)S(1)}, bf16[80,1,512]{2,1,0:T(2,128)(2,1)S(1)}, u32[]{:S(2)}, u32[]{:S(2)}) collective-permute-start(bf16[80,1,512]{2,1,0:T(2,128)(2,1)S(1)} %get-tuple-element.150), channel_id=1, source_target_pairs={{0,4},{4,8},{8,12},{12,16},{16,20},{20,24},{24,28},{1,5},{5,9},{9,... | collective-permute-start | bytes 245768 | tf_op jit(solution)/shard_map/ppermute | solution.py:17
  14.4 7.6 %collective-permute-start.1 = (bf16[80,1,512]{2,1,0:T(2,128)(2,1)S(1)}, bf16[80,1,512]{2,1,0:T(2,128)(2,1)S(1)}, u32[]{:S(2)}, u32[]{:S(2)}) collective-permute-start(bf16[80,1,512]{2,1,0:T(2,128)(2,1)S(1)} %get-tuple-element.151), channel_id=1, source_target_pairs={{4,0},{8,4},{12,8},{16,12},{20,16},{24,20},{28,24},{5,1},{9,5},{13... | collective-permute-start | bytes 245768 | tf_op jit(solution)/shard_map/ppermute | solution.py:18
  31.6 4.8 %copy-start.2 = (f32[256,720]{0,1:T(8,128)S(1)}, f32[256,720]{0,1:T(8,128)}, u32[]{:S(2)}) copy-start(f32[256,720]{0,1:T(8,128)} %custom-call) | copy-start | bytes 2211844
  31.6 4.8 %copy-start.5 = (f32[256]{0:T(256)S(1)}, f32[256]{0:T(256)}, u32[]{:S(2)}) copy-start(f32[256]{0:T(256)} %param.14) | copy-start | bytes 3076
  32.5 4.0 %copy-start.1 = (bf16[16,80,10,130]{3,2,1,0:T(8,128)(2,1)}, bf16[16,80,10,130]{3,2,1,0:T(8,128)(2,1)S(1)}, u32[]{:S(2)}) copy-start(bf16[16,80,10,130]{3,2,1,0:T(8,128)(2,1)S(1)} %fusion.32) | copy-start | bytes 9984004
  36.4 134.2 %copy-start.6 = (u32[32]{0:T(128)S(1)}, u32[32]{0:T(128)}, u32[]{:S(2)}) copy-start(u32[32]{0:T(128)} %constant.46) | copy-start | bytes 388
  37.6 1.0 copy-start.4
  45.9 1.0 copy-start.4
  54.2 1.0 copy-start.4
  62.5 1.0 copy-start.4
  70.8 1.0 copy-start.4
  79.1 1.0 copy-start.4
  87.5 1.0 copy-start.4
  95.8 1.0 copy-start.4
  104.1 1.0 copy-start.4
  112.4 1.0 copy-start.4
  120.7 1.0 copy-start.4
  129.0 1.0 copy-start.4
  137.3 1.0 copy-start.4
  145.6 1.0 copy-start.4
  153.9 1.0 copy-start.4
  162.3 1.0 copy-start.4
  169.4 65.3 %copy-start = (bf16[1,16,64,8,128]{4,3,2,1,0:T(8,128)(2,1)S(1)}, bf16[1,16,64,8,128]{4,3,2,1,0:T(8,128)(2,1)}, u32[]{:S(2)}) copy-start(bf16[1,16,64,8,128]{4,3,2,1,0:T(8,128)(2,1)} %param.10) | copy-start | bytes 6291460
  170.6 96.9 %all-reduce.4.cloned.1.call-start = ((), (), s32[]{:S(2)}) async-start(), calls=%async_computation.2 | async-start | bytes 196608 | tf_op jit(solution)/shard_map/psum | solution.py:119
Sparse Core Ops, SparseCore 0:
  170.7 63.9 reduce-scatter.1
  237.1 30.2 all-reduce.3
where the time goes:
time: 278 us; the launch traced here: 276 us
  waiting for transfers between devices  70.8 us (25%)
  other arithmetic  69.5 us (25%)
  local copies, waits for them, and re-layouts  54.9 us (20%)
  matrix products  31.6 us (11%)
  blocking collectives  25.5 us (9%)
  between operations  14.9 us (5%)
  starting transfers between devices  6.25 us (2%)
    reduce_scatter x1, waiting for transfers between devices, shards(): lax.psum_scatter(grad_weights, 'space', scatter_dimension=0, tiled=True)  62.8 us
    dynamic_update_slice x16, other arithmetic, run_tiles(): return lax.scan(one_tile, grad_init, (windows, cell_olds, out_grads, flags))  27.9 us
    dot_general x16, matrix products, tile_step(): lax.dot_general(gate_grad, patches, (((1,), (1,)), ((), ())), preferred_e...  21.5 us
    unnamed x1, blocking collectives  19.3 us
    squeeze x16, local copies, waits for them, and re-layouts, run_tiles(): return lax.scan(one_tile, grad_init, (windows, cell_olds, out_grads, flags))  18.2 us
    reduce_sum x16, other arithmetic, tile_step(): bias_part = jnp.sum(gate_grad.astype(jnp.float32), axis=1)  12.7 us
    dot_general x16, matrix products, tile_step(): jnp.dot(w_gates, patches, preferred_element_type=jnp.float32)  10.1 us
    dynamic_slice x16, local copies, waits for them, and re-layouts, run_tiles(): return lax.scan(one_tile, grad_init, (windows, cell_olds, out_grads, flags))  9.42 us
  transfers between devices with their start and end apart: 4, of which 4 were waited for; matrix products, arithmetic and copies ran while one was open for 2% of the time, Pallas kernels for 0%

commit v1 on v0

v1 whole, which is shorter than its diff:
```python
import functools

import jax
import jax.numpy as jnp
from jax import lax
from jax.experimental import pallas as pl
from jax.experimental.pallas import tpu as pltpu
from jax.sharding import PartitionSpec as P

TW = 4
MESH = pl.DeviceIdType.MESH
CHUNK = 16


def halo_kernel(n, forcing, hidden, out, f_edge, h_edge, stage, send, landed, in_sem, send_sem, recv_sem):
    _, tiles, in_ch, rows, cols = forcing.shape
    width = in_ch + hidden.shape[2]
    me = lax.axis_index("space")
    loads = []
    for edge, first in ((0, 0), (1, tiles - TW)):
        loads.append(
            (
                pltpu.make_async_copy(
                    forcing.at[0, pl.ds(first, TW)], f_edge.at[edge], in_sem.at[2 * edge]
                ),
                pltpu.make_async_copy(
                    hidden.at[0, pl.ds(first, TW)], h_edge.at[edge], in_sem.at[2 * edge + 1]
                ),
            )
        )
    for pair in loads:
        for copy in pair:
            copy.start()
    barrier = pltpu.get_barrier_semaphore()
    has_up, has_down = me > 0, me < n - 1

    @pl.when(has_up)
    def _():
        pl.semaphore_signal(barrier, inc=1, device_id={"space": me - 1}, device_id_type=MESH)

    @pl.when(has_down)
    def _():
        pl.semaphore_signal(barrier, inc=1, device_id={"space": me + 1}, device_id_type=MESH)

    for edge, row in ((0, 0), (1, rows - 1)):
        for copy in loads[edge]:
            copy.wait()
        for tile in range(TW):
            stage[0 : in_ch * rows] = f_edge[edge, tile].astype(jnp.float32).reshape(in_ch * rows, cols)
            stage[in_ch * rows :] = (
                h_edge[edge, tile].astype(jnp.float32).reshape((width - in_ch) * rows, cols)
            )
            line = stage[pl.ds(row, width, stride=rows), :]
            send[edge, :, tile * cols : (tile + 1) * cols] = line.astype(jnp.bfloat16)

    pl.semaphore_wait(barrier, jnp.where(has_up, 1, 0) + jnp.where(has_down, 1, 0))

    def to_up():
        return pltpu.make_async_remote_copy(
            src_ref=send.at[0], dst_ref=landed.at[1], send_sem=send_sem.at[0],
            recv_sem=recv_sem.at[1], device_id={"space": me - 1}, device_id_type=MESH,
        )

    def to_down():
        return pltpu.make_async_remote_copy(
            src_ref=send.at[1], dst_ref=landed.at[0], send_sem=send_sem.at[1],
            recv_sem=recv_sem.at[0], device_id={"space": me + 1}, device_id_type=MESH,
        )

    @pl.when(has_up)
    def _():
        to_up().start()

    @pl.when(has_down)
    def _():
        to_down().start()

    @pl.when(has_up)
    def _():
        to_up().wait_send()
        to_down().wait_recv()
        out[0] = landed[0]

    @pl.when(jnp.logical_not(has_up))
    def _():
        out[0] = jnp.zeros(out.shape[1:], out.dtype)

    @pl.when(has_down)
    def _():
        to_down().wait_send()
        to_up().wait_recv()
        out[1] = landed[1]

    @pl.when(jnp.logical_not(has_down))
    def _():
        out[1] = jnp.zeros(out.shape[1:], out.dtype)


def exchange_halo(forcing, hidden, n):
    _, tiles, in_ch, rows, cols = forcing.shape
    hid = hidden.shape[2]
    width = in_ch + hid
    edge = (2, width, TW * cols)
    return pl.pallas_call(
        functools.partial(halo_kernel, n),
        out_shape=jax.ShapeDtypeStruct(edge, jnp.bfloat16),
        in_specs=[pl.BlockSpec(memory_space=pl.ANY)] * 2,
        out_specs=pl.BlockSpec(memory_space=pltpu.VMEM),
        scratch_shapes=[
            pltpu.VMEM((2, TW, in_ch, rows, cols), jnp.bfloat16),
            pltpu.VMEM((2, TW, hid, rows, cols), jnp.bfloat16),
            pltpu.VMEM((width * rows, cols), jnp.float32),
            pltpu.VMEM(edge, jnp.bfloat16),
            pltpu.VMEM(edge, jnp.bfloat16),
            pltpu.SemaphoreType.DMA((4,)),
            pltpu.SemaphoreType.DMA((2,)),
            pltpu.SemaphoreType.DMA((2,)),
        ],
        compiler_params=pltpu.CompilerParams(collective_id=0, has_side_effects=True),
        name="halo",
    )(forcing, hidden)


def step_kernel(
    flags, halo, forcing, hidden, cell, grad, w_gates, gate_bias,
    hidden_out, cell_out, acc_out,
    fv, hv, cv, gv, ho, co, field, stage, cs, gs, hs, ns, wbuf, bbuf, pre, gate, bias_acc,
    f_sem, h_sem, c_sem, g_sem, ho_sem, co_sem,
):
    _, tiles, in_ch, rows, cols = forcing.shape
    hid = hidden.shape[2]
    width = in_ch + hid
    bands = tiles // TW
    span = TW * cols
    gates, depth = w_gates.shape
    padded = wbuf.shape[1]
    per = 3 * width

    def load(src, dst, sem, i):
        return pltpu.make_async_copy(
            src.at[0, pl.ds(i * TW, TW)], dst.at[pl.ds(i * TW, TW)], sem.at[i]
        )

    def store(src, dst, sem, i):
        return pltpu.make_async_copy(
            src.at[pl.ds(i * TW, TW)], dst.at[0, pl.ds(i * TW, TW)], sem.at[i]
        )

    for i in range(bands):
        load(forcing, fv, f_sem, i).start()
        load(hidden, hv, h_sem, i).start()
    for i in range(bands):
        load(cell, cv, c_sem, i).start()
        load(grad, gv, g_sem, i).start()

    row = lax.broadcasted_iota(jnp.int32, (gates, 1), 0)
    half = jnp.where(row < 3 * hid, 0.5, 1.0).astype(jnp.float32)
    wbuf[...] = jnp.zeros(wbuf.shape, wbuf.dtype)
    wbuf[:, 0:depth] = (w_gates[...].astype(jnp.float32) * half).astype(wbuf.dtype)
    bbuf[...] = jnp.broadcast_to(gate_bias[...] * half, bbuf.shape)
    acc_out[...] = jnp.zeros(acc_out.shape, acc_out.dtype)
    bias_acc[...] = jnp.zeros(bias_acc.shape, bias_acc.dtype)
    field[(bands * rows + 2) * per :, :] = jnp.zeros((padded - depth, span), field.dtype)

    lane = lax.broadcasted_iota(jnp.int32, (width, span), 1)

    def put_row(line, x):
        base = pl.multiple_of(line * per, 16)
        left = jnp.where(lane == 0, 0.0, pltpu.roll(x, 1, 1))
        right = jnp.where(lane == span - 1, 0.0, pltpu.roll(x, span - 1, 1))
        field[pl.ds(base, width), :] = left.astype(field.dtype)
        field[pl.ds(pl.multiple_of(base + width, 16), width), :] = x.astype(field.dtype)
        field[pl.ds(pl.multiple_of(base + 2 * width, 16), width), :] = right.astype(field.dtype)

    put_row(0, halo[0].astype(jnp.float32))
    put_row(bands * rows + 1, halo[1].astype(jnp.float32))

    @pl.loop(0, bands)
    def _(i):
        load(forcing, fv, f_sem, i).wait()
        load(hidden, hv, h_sem, i).wait()
        for tile in range(TW):
            base = tile * width * rows
            stage[base : base + in_ch * rows] = (
                fv[i * TW + tile].astype(jnp.float32).reshape(in_ch * rows, cols)
            )
            stage[base + in_ch * rows : base + width * rows] = (
                hv[i * TW + tile].astype(jnp.float32).reshape(hid * rows, cols)
            )
        for r in range(rows):
            x = jnp.concatenate(
                [stage[pl.ds(tile * width * rows + r, width, stride=rows), :] for tile in range(TW)],
                axis=1,
            )
            put_row(i * rows + r + 1, x)

    @pl.loop(0, bands)
    def _(i):
        load(cell, cv, c_sem, i).wait()
        load(grad, gv, g_sem, i).wait()
        for tile in range(TW):
            live = jnp.where(flags[i * TW + tile] >= 0, 1.0, 0.0).astype(jnp.float32)
            lines = pl.ds(tile * hid * rows, hid * rows)
            cs[lines] = cv[i * TW + tile].astype(jnp.float32).reshape(hid * rows, cols)
            gs[lines] = gv[i * TW + tile].astype(jnp.float32).reshape(hid * rows, cols) * live
        for r in range(rows):
            start = pl.multiple_of((i * rows + r) * per, 16)
            slot = r % 2
            patches = field[pl.ds(start, padded), :]
            pre[slot] = jnp.dot(wbuf[...], patches, preferred_element_type=jnp.float32)
            for ch in range(0, hid, CHUNK):
                for tile in range(TW):
                    at = pl.ds(tile * hid * rows + ch * rows + r, CHUNK, stride=rows)
                    c0, c1 = tile * cols, (tile + 1) * cols
                    parts = [
                        jnp.tanh(
                            pre[slot, g * hid + ch : g * hid + ch + CHUNK, c0:c1]
                            + bbuf[g * hid + ch : g * hid + ch + CHUNK, :]
                        )
                        for g in range(4)
                    ]
                    t_in, t_forget, t_out, cand = parts
                    in_gate = 0.5 * t_in + 0.5
                    forget = 0.5 * t_forget + 0.5
                    out_gate = 0.5 * t_out + 0.5
                    before = cs[at, :]
                    up = gs[at, :]
                    now = forget * before + in_gate * cand
                    squashed = jnp.tanh(now)
                    hs[at, :] = out_gate * squashed
                    ns[at, :] = now
                    d_cell = up * out_gate * (1.0 - squashed * squashed)
                    grads = (
                        d_cell * cand * (1.0 - t_in * t_in),
                        d_cell * before * (1.0 - t_forget * t_forget),
                        up * squashed * (1.0 - t_out * t_out),
                        d_cell * in_gate * (1.0 - cand * cand),
                    )
                    for g in range(4):
                        lines = slice(g * hid + ch, g * hid + ch + CHUNK)
                        gate[slot, lines, c0:c1] = grads[g].astype(gate.dtype)
                        bias_acc[lines, :] += grads[g]
            acc_out[...] += lax.dot_general(
                gate[slot], patches, (((1,), (1,)), ((), ())), preferred_element_type=jnp.float32
            )
        for tile in range(TW):
            live = flags[i * TW + tile] >= 0
            lines = pl.ds(tile * hid * rows, hid * rows)
            where = i * TW + tile
            keep = jnp.where(live, 1.0, 0.0).astype(jnp.float32)
            alive = jnp.full((hid, rows, cols), keep) > 0.5
            ho[where] = jnp.where(
                alive, hs[lines].reshape(hid, rows, cols), hv[where].astype(jnp.float32)
            ).astype(ho.dtype)
            co[where] = jnp.where(
                alive, ns[lines].reshape(hid, rows, cols), cv[where].astype(jnp.float32)
            ).astype(co.dtype)
        store(ho, hidden_out, ho_sem, i).start()
        store(co, cell_out, co_sem, i).start()

    quarter = jnp.where(row < 3 * hid, 0.25, 1.0).astype(jnp.float32)
    bias_sum = jnp.sum(bias_acc[...], axis=1, keepdims=True) * quarter
    column = lax.broadcasted_iota(jnp.int32, (gates, padded), 1)
    acc_out[...] = jnp.where(
        column < depth, acc_out[...] * quarter, jnp.where(column == depth, bias_sum, 0.0)
    )
    for i in range(bands):
        store(ho, hidden_out, ho_sem, i).wait()
        store(co, cell_out, co_sem, i).wait()


def run_step(flags, halo, forcing, hidden, cell, grad, w_gates, gate_bias):
    _, tiles, in_ch, rows, cols = forcing.shape
    hid = hidden.shape[2]
    width = in_ch + hid
    bands = tiles // TW
    span = TW * cols
    gates, depth = w_gates.shape
    padded = -(-(depth + 1) // 256) * 256
    state = (tiles, hid, rows, cols)
    flat = (TW * hid * rows, cols)
    whole = pl.BlockSpec(memory_space=pl.ANY)
    vmem = pl.BlockSpec(memory_space=pltpu.VMEM)
    return pl.pallas_call(
        step_kernel,
        out_shape=(
            jax.ShapeDtypeStruct(hidden.shape, hidden.dtype),
            jax.ShapeDtypeStruct(cell.shape, cell.dtype),
            jax.ShapeDtypeStruct((gates, padded), jnp.float32),
        ),
        in_specs=[pl.BlockSpec(memory_space=pltpu.SMEM), vmem, whole, whole, whole, whole, vmem, vmem],
        out_specs=(whole, whole, vmem),
        scratch_shapes=[
            pltpu.VMEM((tiles, in_ch, rows, cols), jnp.bfloat16),
            pltpu.VMEM(state, jnp.bfloat16),
            pltpu.VMEM(state, jnp.bfloat16),
            pltpu.VMEM(state, jnp.bfloat16),
            pltpu.VMEM(state, jnp.bfloat16),
            pltpu.VMEM(state, jnp.bfloat16),
            pltpu.VMEM(((bands * rows + 2) * 3 * width + padded - depth, span), jnp.bfloat16),
            pltpu.VMEM((TW * width * rows, cols), jnp.float32),
            pltpu.VMEM(flat, jnp.float32),
            pltpu.VMEM(flat, jnp.float32),
            pltpu.VMEM(flat, jnp.float32),
            pltpu.VMEM(flat, jnp.float32),
            pltpu.VMEM((gates, padded), jnp.bfloat16),
            pltpu.VMEM((gates, cols), jnp.float32),
            pltpu.VMEM((2, gates, span), jnp.float32),
            pltpu.VMEM((2, gates, span), jnp.bfloat16),
            pltpu.VMEM((gates, cols), jnp.float32),
        ]
        + [pltpu.SemaphoreType.DMA((bands,))] * 6,
        compiler_params=pltpu.CompilerParams(vmem_limit_bytes=48 * 1024 * 1024),
        cost_estimate=pl.CostEstimate(
            flops=4 * gates * depth * tiles * rows * cols,
            bytes_accessed=12 * tiles * hid * rows * cols,
            transcendentals=5 * tiles * hid * rows * cols,
        ),
        name="step",
    )(flags, halo, forcing, hidden, cell, grad, w_gates, gate_bias)


def reduce_kernel(n_space, n_dp, acc, out, mine, first, second, part, third, s1, r1, s2, r2, s3, r3):
    sub = out.shape[0] // n_dp
    wide = acc.shape[1] // 2
    home, year = lax.axis_index("space"), lax.axis_index("dp")

    def years_off(off):
        return lax.rem(year + off, n_dp)

    def homes_off(off):
        return lax.rem(home + off, n_space)

    barrier = pltpu.get_barrier_semaphore()
    for off in range(1, n_dp):
        pl.semaphore_signal(barrier, inc=1, device_id={"dp": years_off(off)}, device_id_type=MESH)
    for off in range(1, n_space):
        pl.semaphore_signal(barrier, inc=1, device_id={"space": homes_off(off)}, device_id_type=MESH)

    for d in range(n_dp):
        for s in range(n_space):
            top = (s * n_dp + d) * sub
            mine[d, s] = jnp.concatenate(
                [acc[top : top + sub, 0:wide], acc[top : top + sub, wide:]], axis=0
            ).astype(mine.dtype)

    pl.semaphore_wait(barrier, n_dp + n_space - 2)

    copies = []
    for off in range(1, n_dp):
        copies.append(
            pltpu.make_async_remote_copy(
                src_ref=mine.at[years_off(off)], dst_ref=first.at[off - 1], send_sem=s1.at[off - 1],
                recv_sem=r1.at[off - 1], device_id={"dp": years_off(off)}, device_id_type=MESH,
            )
        )
        copies[-1].start()
    for copy in copies:
        copy.wait()
    total = mine[year].astype(jnp.float32)
    for off in range(1, n_dp):
        total = total + first[off - 1].astype(jnp.float32)
    part[...] = total.astype(part.dtype)

    copies = []
    for off in range(1, n_space):
        copies.append(
            pltpu.make_async_remote_copy(
                src_ref=part.at[homes_off(off)], dst_ref=second.at[off - 1], send_sem=s2.at[off - 1],
                recv_sem=r2.at[off - 1], device_id={"space": homes_off(off)}, device_id_type=MESH,
            )
        )
        copies[-1].start()
    for copy in copies:
        copy.wait()
    total = part[home].astype(jnp.float32)
    for off in range(1, n_space):
        total = total + second[off - 1].astype(jnp.float32)
    third[0] = total

    copies = []
    for off in range(1, n_dp):
        copies.append(
            pltpu.make_async_remote_copy(
                src_ref=third.at[0], dst_ref=third.at[off], send_sem=s3.at[off - 1],
                recv_sem=r3.at[off - 1], device_id={"dp": years_off(off)}, device_id_type=MESH,
            )
        )
        copies[-1].start()
    for copy in copies:
        copy.wait()
    for off in range(n_dp):
        whose = lax.rem(year - off + n_dp, n_dp)
        lines = pl.ds(pl.multiple_of(whose * sub, 8), sub)
        out[lines, 0:wide] = third[off, 0:sub, :]
        out[lines, wide:] = third[off, sub:, :]


def reduce_all(acc, n_space, n_dp):
    gates, padded = acc.shape
    keep = gates // n_space
    sub = keep // n_dp
    block = (2 * sub, padded // 2)
    vmem = pl.BlockSpec(memory_space=pltpu.VMEM)
    return pl.pallas_call(
        functools.partial(reduce_kernel, n_space, n_dp),
        out_shape=jax.ShapeDtypeStruct((keep, padded), jnp.float32),
        in_specs=[vmem],
        out_specs=vmem,
        scratch_shapes=[
            pltpu.VMEM((n_dp, n_space) + block, jnp.bfloat16),
            pltpu.VMEM((n_dp - 1, n_space) + block, jnp.bfloat16),
            pltpu.VMEM((n_space - 1,) + block, jnp.bfloat16),
            pltpu.VMEM((n_space,) + block, jnp.bfloat16),
            pltpu.VMEM((n_dp,) + block, jnp.float32),
            pltpu.SemaphoreType.DMA((n_dp - 1,)),
            pltpu.SemaphoreType.DMA((n_dp - 1,)),
            pltpu.SemaphoreType.DMA((n_space - 1,)),
            pltpu.SemaphoreType.DMA((n_space - 1,)),
            pltpu.SemaphoreType.DMA((n_dp - 1,)),
            pltpu.SemaphoreType.DMA((n_dp - 1,)),
        ],
        compiler_params=pltpu.CompilerParams(collective_id=1, has_side_effects=True),
        name="reduce",
    )(acc)


def shards(n_space, n_dp, forcing, hidden_prev, cell_prev, hidden_grad, w_gates, gate_bias, worker):
    tiles = forcing.shape[1]
    gates, depth = w_gates.shape
    mine = lax.dynamic_slice_in_dim(worker[0], lax.axis_index("space") * tiles, tiles)
    halo = exchange_halo(forcing, hidden_prev, n_space)
    hidden_next, cell_next, acc = run_step(
        mine, halo, forcing, hidden_prev, cell_prev, hidden_grad, w_gates, gate_bias[:, None]
    )
    if gates % (8 * n_space * n_dp) == 0:
        total = reduce_all(acc, n_space, n_dp)
    else:
        total = lax.psum_scatter(acc, "space", scatter_dimension=0, tiled=True)
        total = lax.psum(total, "dp")
    return hidden_next, cell_next, total[:, :depth], total[:, depth]


def solution(mesh):
    state = P("dp", "space", None, None, None)
    return jax.shard_map(
        functools.partial(shards, mesh.shape["space"], mesh.shape["dp"]),
        mesh=mesh,
        in_specs=(state, state, state, state, P(), P(), P("dp", None)),
        out_specs=(state, state, P("space", None), P("space")),
        check_vma=False,
    )
```

time: 278 us -> 66.6 us (0.24)
  waiting for transfers between devices: 70.8 us -> 0 us
  other arithmetic: 69.5 us -> 0 us
  Pallas kernels: 0 us -> 56.4 us
  local copies, waits for them, and re-layouts: 54.9 us -> 9.08 us
  matrix products: 31.6 us -> 0 us
  blocking collectives: 25.5 us -> 0 us
  between operations: 14.9 us -> 0.73 us
  starting transfers between devices: 6.25 us -> 0 us
    reduce_scatter x1 -> x0, waiting for transfers between devices: 62.8 us -> none  [shards(): lax.psum_scatter(grad_weights, 'space', scatter_dimension=0, tiled=True)]
    pallas_call x0 -> x3, Pallas kernels: none -> 56.4 us  [the longest x1 29.5 us: run_step(): pl.pallas_call(step_kernel, out_shape=(jax.ShapeDtypeStruct(hidden.shape,...]
    dot_general x32 -> x0, matrix products: 31.6 us -> none  [the longest x16 21.5 us: tile_step(): lax.dot_general(gate_grad, patches, (((1,), (1,)), ((), ())), preferred_e...]
    dynamic_update_slice x16 -> x0, other arithmetic: 27.9 us -> none  [run_tiles(): return lax.scan(one_tile, grad_init, (windows, cell_olds, out_grads, flags))]
    unnamed x1 -> x0, blocking collectives: 19.3 us -> none
    squeeze x16 -> x0, local copies, waits for them, and re-layouts: 18.2 us -> none  [run_tiles(): return lax.scan(one_tile, grad_init, (windows, cell_olds, out_grads, flags))]
    reduce_sum x16 -> x0, other arithmetic: 12.7 us -> none  [tile_step(): bias_part = jnp.sum(gate_grad.astype(jnp.float32), axis=1)]
    while x209 -> x0, local copies, waits for them, and re-layouts: 10.5 us -> none
  transfers between devices with their start and end apart: 4 -> 0, of which waited for: 4 -> 0; matrix products, arithmetic and copies ran while one was open for 2% -> 0% of each run, Pallas kernels for 0% -> 0%
where the time goes in v1:
time: 66.6 us; the launch traced here: 66.2 us
  Pallas kernels  56.4 us (85%)
  local copies, waits for them, and re-layouts  9.08 us (14%)
  between operations  0.73 us (1%)
    pallas_call x1, Pallas kernels, run_step(): pl.pallas_call(step_kernel, out_shape=(jax.ShapeDtypeStruct(hidden.shape,...  29.5 us
    pallas_call x1, Pallas kernels, reduce_all(): pl.pallas_call(functools.partial(reduce_kernel, n_space, n_dp), out_shape...  19.2 us
    pallas_call x1, Pallas kernels, exchange_halo(): pl.pallas_call(functools.partial(halo_kernel, n), out_shape=jax.ShapeDtyp...  7.65 us
    unnamed x14, local copies, waits for them, and re-layouts  6.72 us
    slice x1, local copies, waits for them, and re-layouts, shards(): return (hidden_next, cell_next, total[:, :depth], total[:, depth])  1.41 us

profile of v1, /device:TPU:0, one launch (start us, length us, event | category | flops | bytes accessed | tf_op | source)
XLA Modules:
  0.0 66.2 jit_solution(4282704980624172400)
XLA Ops:
  0.6 0.0 copy-start
  0.6 0.0 copy-start.1
  0.7 0.0 copy-start.3
  0.7 0.6 copy-done
  1.3 0.1 dynamic-slice_bitcast_fusion.flags
  1.4 0.9 %copy.13.gate_bias = f32[256,1]{1,0:T(8,128)S(1)} copy(f32[256,1]{0,1:T(1,128)} %bitcast.5) | data formatting | bytes 2048 | tf_op jit(solution)/shard_map/broadcast_in_dim | solution.py:434
  2.3 7.7 %halo.1 = bf16[2,80,512]{2,1,0:T(8,128)(2,1)} custom-call(bf16[1,16,16,8,128]{4,3,2,1,0:T(8,128)(2,1)} %forcing.3, bf16[1,16,64,8,128]{4,3,2,1,0:T(8,128)(2,1)} %hidden.3), custom_call_target="tpu_custom_call" | custom-call | tf_op jit(solution)/shard_map/halo/pallas_call | solution.py:104
  9.9 1.2 %copy.12.w_gates = bf16[256,720]{1,0:T(8,128)(2,1)S(1)} copy(bf16[256,720]{0,1:T(8,128)(2,1)} %param.11) | data formatting | bytes 737280 | tf_op args[4]
  11.1 0.0 copy-done.1
  11.1 0.0 copy-done.3
  11.1 0.0 copy-start.4
  11.1 0.9 %copy-done.4 = bf16[2,80,512]{2,1,0:T(8,128)(2,1)S(1)} copy-done((bf16[2,80,512]{2,1,0:T(8,128)(2,1)S(1)}, bf16[2,80,512]{2,1,0:T(8,128)(2,1)}, u32[]{:S(2)}) %copy-start.4) | copy-done | bytes 163864
  12.0 0.0 copy-start.5
  12.0 1.6 %copy-done.5 = bf16[1,16,64,8,128]{4,3,2,1,0:T(8,128)(2,1)S(1)} copy-done((bf16[1,16,64,8,128]{4,3,2,1,0:T(8,128)(2,1)S(1)}, bf16[1,16,64,8,128]{4,3,2,1,0:T(8,128)(2,1)}, u32[]{:S(2)}) %copy-start.5) | copy-done | bytes 2097176
  13.6 29.5 %step.1 = (bf16[1,16,64,8,128]{4,3,2,1,0:T(8,128)(2,1)}, bf16[1,16,64,8,128]{4,3,2,1,0:T(8,128)(2,1)}, f32[256,768]{1,0:T(8,128)S(1)}) custom-call(s32[16]{0:T(128)S(1)} %dynamic-slice_bitcast_fusion.flags, bf16[2,80,512]{2,1,0:T(8,128)(2,1)S(1)} %copy-done.4, bf16[1,16,16,8,128]{4,3,2,1,0:T(8,128)(2,1)S(1)} %copy-done.3, ...), custom_call_target="tpu_custom_call" | custom-call | flops 12079595520 | bytes 12582912 | tf_op jit(solution)/shard_map/step/pallas_call | solution.py:284
  43.2 0.0 copy-start.2
  43.2 0.9 %copy-done.2 = f32[256,768]{1,0:T(8,128)} copy-done((f32[256,768]{1,0:T(8,128)}, f32[256,768]{1,0:T(8,128)S(1)}, u32[]{:S(2)}) %copy-start.2) | copy-done | bytes 786456
  44.1 19.2 %reduce.3 = f32[32,768]{1,0:T(8,128)} custom-call(f32[256,768]{1,0:T(8,128)} %copy-done.2), custom_call_target="tpu_custom_call" | custom-call | tf_op jit(solution)/shard_map/reduce/pallas_call | solution.py:405
  63.3 1.4 %slice_reduce_fusion = f32[32]{0:T(128)} fusion(f32[32,768]{1,0:T(8,128)} %reduce.3), kind=kLoop, calls=%fused_computation | loop fusion | bytes 256 | tf_op jit(solution)/shard_map/slice | solution.py:441
  64.7 1.5 %copy.15 = f32[32,720]{1,0:T(8,128)} copy(f32[32,720]{1,0:T(8,128)} %bitcast.4) | data formatting | bytes 184320
Async XLA Ops:
  0.6 0.7 copy-start
  0.6 10.4 %copy-start.1 = (bf16[1,16,64,8,128]{4,3,2,1,0:T(8,128)(2,1)S(1)}, bf16[1,16,64,8,128]{4,3,2,1,0:T(8,128)(2,1)}, u32[]{:S(2)}) copy-start(bf16[1,16,64,8,128]{4,3,2,1,0:T(8,128)(2,1)} %hidden.3) | copy-start | bytes 6291460
  0.7 10.4 %copy-start.3 = (bf16[1,16,16,8,128]{4,3,2,1,0:T(8,128)(2,1)S(1)}, bf16[1,16,16,8,128]{4,3,2,1,0:T(8,128)(2,1)}, u32[]{:S(2)}) copy-start(bf16[1,16,16,8,128]{4,3,2,1,0:T(8,128)(2,1)} %forcing.3) | copy-start | bytes 1572868
  11.1 0.9 %copy-start.4 = (bf16[2,80,512]{2,1,0:T(8,128)(2,1)S(1)}, bf16[2,80,512]{2,1,0:T(8,128)(2,1)}, u32[]{:S(2)}) copy-start(bf16[2,80,512]{2,1,0:T(8,128)(2,1)} %halo.1) | copy-start | bytes 491524
  12.0 1.6 %copy-start.5 = (bf16[1,16,64,8,128]{4,3,2,1,0:T(8,128)(2,1)S(1)}, bf16[1,16,64,8,128]{4,3,2,1,0:T(8,128)(2,1)}, u32[]{:S(2)}) copy-start(bf16[1,16,64,8,128]{4,3,2,1,0:T(8,128)(2,1)} %cell.1) | copy-start | bytes 6291460
  43.2 0.9 %copy-start.2 = (f32[256,768]{1,0:T(8,128)}, f32[256,768]{1,0:T(8,128)S(1)}, u32[]{:S(2)}) copy-start(f32[256,768]{1,0:T(8,128)S(1)} %get-tuple-element.9.acc) | copy-start | bytes 2359300

commit v2 on v1

--- a/solution.py
+++ b/solution.py
@@ -10,6 +10,7 @@
 TW = 4
 MESH = pl.DeviceIdType.MESH
 CHUNK = 16
+GROUP = 4
 
 
 def halo_kernel(n, forcing, hidden, out, f_edge, h_edge, stage, send, landed, in_sem, send_sem, recv_sem):
@@ -123,18 +124,21 @@
 
 def step_kernel(
     flags, halo, forcing, hidden, cell, grad, w_gates, gate_bias,
-    hidden_out, cell_out, acc_out,
+    hidden_out, cell_out, sums_out,
     fv, hv, cv, gv, ho, co, field, stage, cs, gs, hs, ns, wbuf, bbuf, pre, gate, bias_acc,
-    f_sem, h_sem, c_sem, g_sem, ho_sem, co_sem,
+    edges, wt, acc, sums, f_sem, h_sem, c_sem, g_sem, ho_sem, co_sem, x_sem,
 ):
     _, tiles, in_ch, rows, cols = forcing.shape
     hid = hidden.shape[2]
     width = in_ch + hid
     bands = tiles // TW
     span = TW * cols
-    gates, depth = w_gates.shape
+    depth, gates = w_gates.shape
     padded = wbuf.shape[1]
     per = 3 * width
+    get_edges = pltpu.make_async_copy(halo, edges, x_sem.at[0])
+    get_weights = pltpu.make_async_copy(w_gates, wt.at[pl.ds(0, depth)], x_sem.at[1])
+    put_sums = pltpu.make_async_copy(sums, sums_out, x_sem.at[2])
 
     def load(src, dst, sem, i):
         return pltpu.make_async_copy(
@@ -149,16 +153,17 @@
     for i in range(bands):
         load(forcing, fv, f_sem, i).start()
         load(hidden, hv, h_sem, i).start()
+    get_weights.start()
+    get_edges.start()
     for i in range(bands):
         load(cell, cv, c_sem, i).start()
         load(grad, gv, g_sem, i).start()
 
     row = lax.broadcasted_iota(jnp.int32, (gates, 1), 0)
     half = jnp.where(row < 3 * hid, 0.5, 1.0).astype(jnp.float32)
-    wbuf[...] = jnp.zeros(wbuf.shape, wbuf.dtype)
-    wbuf[:, 0:depth] = (w_gates[...].astype(jnp.float32) * half).astype(wbuf.dtype)
-    bbuf[...] = jnp.broadcast_to(gate_bias[...] * half, bbuf.shape)
-    acc_out[...] = jnp.zeros(acc_out.shape, acc_out.dtype)
+    wt[depth:, :] = jnp.zeros((padded - depth, gates), wt.dtype)
+    bbuf[...] = jnp.broadcast_to(gate_bias[...], (cols, gates)).T * half
+    acc[...] = jnp.zeros(acc.shape, acc.dtype)
     bias_acc[...] = jnp.zeros(bias_acc.shape, bias_acc.dtype)
     field[(bands * rows + 2) * per :, :] = jnp.zeros((padded - depth, span), field.dtype)
 
@@ -171,9 +176,6 @@
         field[pl.ds(base, width), :] = left.astype(field.dtype)
         field[pl.ds(pl.multiple_of(base + width, 16), width), :] = x.astype(field.dtype)
         field[pl.ds(pl.multiple_of(base + 2 * width, 16), width), :] = right.astype(field.dtype)
-
-    put_row(0, halo[0].astype(jnp.float32))
-    put_row(bands * rows + 1, halo[1].astype(jnp.float32))
 
     @pl.loop(0, bands)
     def _(i):
@@ -194,32 +196,41 @@
             )
             put_row(i * rows + r + 1, x)
 
+    get_weights.wait()
+    wbuf[...] = (wt[...].astype(jnp.float32).T * half).astype(wbuf.dtype)
+    get_edges.wait()
+    put_row(0, edges[0].astype(jnp.float32))
+    put_row(bands * rows + 1, edges[1].astype(jnp.float32))
+
     @pl.loop(0, bands)
     def _(i):
         load(cell, cv, c_sem, i).wait()
         load(grad, gv, g_sem, i).wait()
-        for tile in range(TW):
-            live = jnp.where(flags[i * TW + tile] >= 0, 1.0, 0.0).astype(jnp.float32)
-            lines = pl.ds(tile * hid * rows, hid * rows)
-            cs[lines] = cv[i * TW + tile].astype(jnp.float32).reshape(hid * rows, cols)
-            gs[lines] = gv[i * TW + tile].astype(jnp.float32).reshape(hid * rows, cols) * live
-        for r in range(rows):
-            start = pl.multiple_of((i * rows + r) * per, 16)
-            slot = r % 2
-            patches = field[pl.ds(start, padded), :]
-            pre[slot] = jnp.dot(wbuf[...], patches, preferred_element_type=jnp.float32)
+
+        def patches(r):
+            return field[pl.ds(pl.multiple_of((i * rows + r) * per, 16), padded), :]
+
+        def forward(r):
+            pre[r % 2] = jnp.dot(wbuf[...], patches(r), preferred_element_type=jnp.float32)
+
+        def backward(group):
+            seen = jnp.concatenate([patches(r) for r in range(group * GROUP, (group + 1) * GROUP)], axis=1)
+            acc[...] += lax.dot_general(
+                seen, gate[group % 2], (((1,), (1,)), ((), ())), preferred_element_type=jnp.float32
+            )
+
+        def pointwise(r):
+            slot, group = r % 2, r // GROUP
             for ch in range(0, hid, CHUNK):
+                lines = [slice(g * hid + ch, g * hid + ch + CHUNK) for g in range(4)]
+                bias = [bbuf[lines[g], :] for g in range(4)]
+                totals = [None] * 4
                 for tile in range(TW):
                     at = pl.ds(tile * hid * rows + ch * rows + r, CHUNK, stride=rows)
                     c0, c1 = tile * cols, (tile + 1) * cols
-                    parts = [
-                        jnp.tanh(
-                            pre[slot, g * hid + ch : g * hid + ch + CHUNK, c0:c1]
-                            + bbuf[g * hid + ch : g * hid + ch + CHUNK, :]
-                        )
-                        for g in range(4)
+                    t_in, t_forget, t_out, cand = [
+                        jnp.tanh(pre[slot, lines[g], c0:c1] + bias[g]) for g in range(4)
                     ]
-                    t_in, t_forget, t_out, cand = parts
                     in_gate = 0.5 * t_in + 0.5
                     forget = 0.5 * t_forget + 0.5
                     out_gate = 0.5 * t_out + 0.5
@@ -236,13 +247,26 @@
                         up * squashed * (1.0 - t_out * t_out),
                         d_cell * in_gate * (1.0 - cand * cand),
                     )
+                    d0 = (r % GROUP) * span + c0
                     for g in range(4):
-                        lines = slice(g * hid + ch, g * hid + ch + CHUNK)
-                        gate[slot, lines, c0:c1] = grads[g].astype(gate.dtype)
-                        bias_acc[lines, :] += grads[g]
-            acc_out[...] += lax.dot_general(
-                gate[slot], patches, (((1,), (1,)), ((), ())), preferred_element_type=jnp.float32
-            )
+                        gate[group % 2, lines[g], d0 : d0 + cols] = grads[g].astype(gate.dtype)
+                        totals[g] = grads[g] if totals[g] is None else totals[g] + grads[g]
+                for g in range(4):
+                    bias_acc[lines[g], :] += totals[g]
+
+        forward(0)
+        for tile in range(TW):
+            live = jnp.where(flags[i * TW + tile] >= 0, 1.0, 0.0).astype(jnp.float32)
+            lines = pl.ds(tile * hid * rows, hid * rows)
+            cs[lines] = cv[i * TW + tile].astype(jnp.float32).reshape(hid * rows, cols)
+            gs[lines] = gv[i * TW + tile].astype(jnp.float32).reshape(hid * rows, cols) * live
+        for r in range(rows):
+            if r + 1 < rows:
+                forward(r + 1)
+            if r % GROUP == 0 and r > 0:
+                backward(r // GROUP - 1)
+            pointwise(r)
+        backward(rows // GROUP - 1)
         for tile in range(TW):
             live = flags[i * TW + tile] >= 0
             lines = pl.ds(tile * hid * rows, hid * rows)
@@ -261,21 +285,34 @@
     quarter = jnp.where(row < 3 * hid, 0.25, 1.0).astype(jnp.float32)
     bias_sum = jnp.sum(bias_acc[...], axis=1, keepdims=True) * quarter
     column = lax.broadcasted_iota(jnp.int32, (gates, padded), 1)
-    acc_out[...] = jnp.where(
-        column < depth, acc_out[...] * quarter, jnp.where(column == depth, bias_sum, 0.0)
+    done = jnp.where(
+        column < depth, acc[...].T * quarter, jnp.where(column == depth, bias_sum, 0.0)
     )
+    if len(sums.shape) == 2:
+        sums[...] = done
+    else:
+        n_dp, n_space = sums.shape[:2]
+        sub, wide = gates // (n_dp * n_space), padded // 2
+        for d in range(n_dp):
+            for s in range(n_space):
+                top = (s * n_dp + d) * sub
+                sums[d, s] = jnp.concatenate(
+                    [done[top : top + sub, 0:wide], done[top : top + sub, wide:]], axis=0
+                ).astype(sums.dtype)
+    put_sums.start()
+    put_sums.wait()
     for i in range(bands):
         store(ho, hidden_out, ho_sem, i).wait()
         store(co, cell_out, co_sem, i).wait()
 
 
-def run_step(flags, halo, forcing, hidden, cell, grad, w_gates, gate_bias):
+def run_step(sums, flags, halo, forcing, hidden, cell, grad, w_gates, gate_bias):
     _, tiles, in_ch, rows, cols = forcing.shape
     hid = hidden.shape[2]
     width = in_ch + hid
     bands = tiles // TW
     span = TW * cols
-    gates, depth = w_gates.shape
+    depth, gates = w_gates.shape
     padded = -(-(depth + 1) // 256) * 256
     state = (tiles, hid, rows, cols)
     flat = (TW * hid * rows, cols)
@@ -286,10 +323,10 @@
         out_shape=(
             jax.ShapeDtypeStruct(hidden.shape, hidden.dtype),
             jax.ShapeDtypeStruct(cell.shape, cell.dtype),
-            jax.ShapeDtypeStruct((gates, padded), jnp.float32),
+            sums,
         ),
-        in_specs=[pl.BlockSpec(memory_space=pltpu.SMEM), vmem, whole, whole, whole, whole, vmem, vmem],
-        out_specs=(whole, whole, vmem),
+        in_specs=[pl.BlockSpec(memory_space=pltpu.SMEM), whole, whole, whole, whole, whole, whole, vmem],
+        out_specs=(whole, whole, whole),
         scratch_shapes=[
             pltpu.VMEM((tiles, in_ch, rows, cols), jnp.bfloat16),
             pltpu.VMEM(state, jnp.bfloat16),
@@ -306,11 +343,16 @@
             pltpu.VMEM((gates, padded), jnp.bfloat16),
             pltpu.VMEM((gates, cols), jnp.float32),
             pltpu.VMEM((2, gates, span), jnp.float32),
-            pltpu.VMEM((2, gates, span), jnp.bfloat16),
+            pltpu.VMEM((2, gates, GROUP * span), jnp.bfloat16),
             pltpu.VMEM((gates, cols), jnp.float32),
+            pltpu.VMEM(halo.shape, halo.dtype),
+            pltpu.VMEM((padded, gates), jnp.bfloat16),
+            pltpu.VMEM((padded, gates), jnp.float32),
+            pltpu.VMEM(sums.shape, sums.dtype),
         ]
-        + [pltpu.SemaphoreType.DMA((bands,))] * 6,
-        compiler_params=pltpu.CompilerParams(vmem_limit_bytes=48 * 1024 * 1024),
+        + [pltpu.SemaphoreType.DMA((bands,))] * 6
+        + [pltpu.SemaphoreType.DMA((3,))],
+        compiler_params=pltpu.CompilerParams(vmem_limit_bytes=60 * 1024 * 1024),
         cost_estimate=pl.CostEstimate(
             flops=4 * gates * depth * tiles * rows * cols,
             bytes_accessed=12 * tiles * hid * rows * cols,
@@ -320,9 +362,9 @@
     )(flags, halo, forcing, hidden, cell, grad, w_gates, gate_bias)
 
 
-def reduce_kernel(n_space, n_dp, acc, out, mine, first, second, part, third, s1, r1, s2, r2, s3, r3):
+def reduce_kernel(n_space, n_dp, sums, out, mine, first, second, part, third, own, s1, r1, s2, r2, s3, r3):
     sub = out.shape[0] // n_dp
-    wide = acc.shape[1] // 2
+    wide = sums.shape[-1]
     home, year = lax.axis_index("space"), lax.axis_index("dp")
 
     def years_off(off):
@@ -330,91 +372,88 @@
 
     def homes_off(off):
         return lax.rem(home + off, n_space)
+
+    def over_years(off, place):
+        return pltpu.make_async_remote_copy(
+            src_ref=sums.at[years_off(off), homes_off(place)], dst_ref=first.at[off - 1, place],
+            send_sem=s1.at[off - 1, place], recv_sem=r1.at[off - 1, place],
+            device_id={"dp": years_off(off)}, device_id_type=MESH,
+        )
+
+    def over_homes(off):
+        return pltpu.make_async_remote_copy(
+            src_ref=part.at[off], dst_ref=second.at[off - 1], send_sem=s2.at[off - 1],
+            recv_sem=r2.at[off - 1], device_id={"space": homes_off(off)}, device_id_type=MESH,
+        )
+
+    def to_years(off):
+        return pltpu.make_async_remote_copy(
+            src_ref=third.at[0], dst_ref=third.at[off], send_sem=s3.at[off - 1],
+            recv_sem=r3.at[off - 1], device_id={"dp": years_off(off)}, device_id_type=MESH,
+        )
 
     barrier = pltpu.get_barrier_semaphore()
     for off in range(1, n_dp):
         pl.semaphore_signal(barrier, inc=1, device_id={"dp": years_off(off)}, device_id_type=MESH)
     for off in range(1, n_space):
         pl.semaphore_signal(barrier, inc=1, device_id={"space": homes_off(off)}, device_id_type=MESH)
-
-    for d in range(n_dp):
-        for s in range(n_space):
-            top = (s * n_dp + d) * sub
-            mine[d, s] = jnp.concatenate(
-                [acc[top : top + sub, 0:wide], acc[top : top + sub, wide:]], axis=0
-            ).astype(mine.dtype)
-
+    get_mine = pltpu.make_async_copy(sums.at[year], mine, own)
+    get_mine.start()
     pl.semaphore_wait(barrier, n_dp + n_space - 2)
 
-    copies = []
-    for off in range(1, n_dp):
-        copies.append(
-            pltpu.make_async_remote_copy(
-                src_ref=mine.at[years_off(off)], dst_ref=first.at[off - 1], send_sem=s1.at[off - 1],
-                recv_sem=r1.at[off - 1], device_id={"dp": years_off(off)}, device_id_type=MESH,
-            )
-        )
-        copies[-1].start()
-    for copy in copies:
-        copy.wait()
-    total = mine[year].astype(jnp.float32)
-    for off in range(1, n_dp):
-        total = total + first[off - 1].astype(jnp.float32)
-    part[...] = total.astype(part.dtype)
-
-    copies = []
+    order = list(range(1, n_space)) + [0]
+    for place in order:
+        for off in range(1, n_dp):
+            over_years(off, place).start()
+    get_mine.wait()
+    for place in order:
+        total = mine[homes_off(place)].astype(jnp.float32)
+        for off in range(1, n_dp):
+            over_years(off, place).wait_recv()
+            total = total + first[off - 1, place].astype(jnp.float32)
+        if place:
+            part[place] = total.astype(part.dtype)
+            over_homes(place).start()
     for off in range(1, n_space):
-        copies.append(
-            pltpu.make_async_remote_copy(
-                src_ref=part.at[homes_off(off)], dst_ref=second.at[off - 1], send_sem=s2.at[off - 1],
-                recv_sem=r2.at[off - 1], device_id={"space": homes_off(off)}, device_id_type=MESH,
-            )
-        )
-        copies[-1].start()
-    for copy in copies:
-        copy.wait()
-    total = part[home].astype(jnp.float32)
-    for off in range(1, n_space):
+        over_homes(off).wait_recv()
         total = total + second[off - 1].astype(jnp.float32)
     third[0] = total
-
-    copies = []
     for off in range(1, n_dp):
-        copies.append(
-            pltpu.make_async_remote_copy(
-                src_ref=third.at[0], dst_ref=third.at[off], send_sem=s3.at[off - 1],
-                recv_sem=r3.at[off - 1], device_id={"dp": years_off(off)}, device_id_type=MESH,
-            )
-        )
-        copies[-1].start()
-    for copy in copies:
-        copy.wait()
+        to_years(off).start()
     for off in range(n_dp):
+        if off:
+            to_years(off).wait_recv()
         whose = lax.rem(year - off + n_dp, n_dp)
         lines = pl.ds(pl.multiple_of(whose * sub, 8), sub)
         out[lines, 0:wide] = third[off, 0:sub, :]
         out[lines, wide:] = third[off, sub:, :]
-
-
-def reduce_all(acc, n_space, n_dp):
-    gates, padded = acc.shape
+    for place in order:
+        for off in range(1, n_dp):
+            over_years(off, place).wait_send()
+    for off in range(1, n_space):
+        over_homes(off).wait_send()
+    for off in range(1, n_dp):
+        to_years(off).wait_send()
+
+
+def reduce_all(sums, gates):
+    n_dp, n_space, _, wide = sums.shape
     keep = gates // n_space
-    sub = keep // n_dp
-    block = (2 * sub, padded // 2)
-    vmem = pl.BlockSpec(memory_space=pltpu.VMEM)
+    block = sums.shape[2:]
     return pl.pallas_call(
         functools.partial(reduce_kernel, n_space, n_dp),
-        out_shape=jax.ShapeDtypeStruct((keep, padded), jnp.float32),
-        in_specs=[vmem],
-        out_specs=vmem,
+        out_shape=jax.ShapeDtypeStruct((keep, 2 * wide), jnp.float32),
+        in_specs=[pl.BlockSpec(memory_space=pl.ANY)],
+        out_specs=pl.BlockSpec(memory_space=pltpu.VMEM),
         scratch_shapes=[
-            pltpu.VMEM((n_dp, n_space) + block, jnp.bfloat16),
+            pltpu.VMEM((n_space,) + block, jnp.bfloat16),
             pltpu.VMEM((n_dp - 1, n_space) + block, jnp.bfloat16),
             pltpu.VMEM((n_space - 1,) + block, jnp.bfloat16),
             pltpu.VMEM((n_space,) + block, jnp.bfloat16),
             pltpu.VMEM((n_dp,) + block, jnp.float32),
-            pltpu.SemaphoreType.DMA((n_dp - 1,)),
-            pltpu.SemaphoreType.DMA((n_dp - 1,)),
+            pltpu.SemaphoreType.DMA,
+            pltpu.SemaphoreType.DMA((n_dp - 1, n_space)),
+            pltpu.SemaphoreType.DMA((n_dp - 1, n_space)),
             pltpu.SemaphoreType.DMA((n_space - 1,)),
             pltpu.SemaphoreType.DMA((n_space - 1,)),
             pltpu.SemaphoreType.DMA((n_dp - 1,)),
@@ -422,7 +461,7 @@
         ],
         compiler_params=pltpu.CompilerParams(collective_id=1, has_side_effects=True),
         name="reduce",
-    )(acc)
+    )(sums)
 
 
 def shards(n_space, n_dp, forcing, hidden_prev, cell_prev, hidden_grad, w_gates, gate_bias, worker):
@@ -430,14 +469,19 @@
     gates, depth = w_gates.shape
     mine = lax.dynamic_slice_in_dim(worker[0], lax.axis_index("space") * tiles, tiles)
     halo = exchange_halo(forcing, hidden_prev, n_space)
-    hidden_next, cell_next, acc = run_step(
-        mine, halo, forcing, hidden_prev, cell_prev, hidden_grad, w_gates, gate_bias[:, None]
+    padded = -(-(depth + 1) // 256) * 256
+    sub, ragged = divmod(gates, n_space * n_dp)
+    staged = ragged == 0 and sub % 8 == 0
+    sums = jax.ShapeDtypeStruct((gates, padded), jnp.float32)
+    if staged:
+        sums = jax.ShapeDtypeStruct((n_dp, n_space, 2 * sub, padded // 2), jnp.bfloat16)
+    hidden_next, cell_next, sums = run_step(
+        sums, mine, halo, forcing, hidden_prev, cell_prev, hidden_grad, w_gates.T, gate_bias[None, :]
     )
-    if gates % (8 * n_space * n_dp) == 0:
-        total = reduce_all(acc, n_space, n_dp)
+    if staged:
+        total = reduce_all(sums, gates)
     else:
-        total = lax.psum_scatter(acc, "space", scatter_dimension=0, tiled=True)
-        total = lax.psum(total, "dp")
+        total = lax.psum(lax.psum_scatter(sums, "space", scatter_dimension=0, tiled=True), "dp")
     return hidden_next, cell_next, total[:, :depth], total[:, depth]
 
 

time: 66.6 us -> 58.5 us (0.88)
  local copies, waits for them, and re-layouts: 9.08 us -> 4.18 us
  Pallas kernels: 56.4 us -> 53.4 us
    unnamed x14 -> x3, local copies, waits for them, and re-layouts: 6.72 us -> 2.19 us
    pallas_call x1, Pallas kernels: 29.5 us -> 27.6 us  [run_step(): pl.pallas_call(step_kernel, out_shape=(jax.ShapeDtypeStruct(hidden.shape,...]
    pallas_call x1, Pallas kernels: 19.2 us -> 18.1 us  [reduce_all(): pl.pallas_call(functools.partial(reduce_kernel, n_space, n_dp), out_shape...]
    broadcast_in_dim x1 -> x0, local copies, waits for them, and re-layouts: 0.88 us -> none  [shards(): gate_bias[:, None]]
where the time goes in v2:
time: 58.5 us; the launch traced here: 58.2 us
  Pallas kernels  53.4 us (91%)
  local copies, waits for them, and re-layouts  4.18 us (7%)
  between operations  0.67 us (1%)
    pallas_call x1, Pallas kernels, run_step(): pl.pallas_call(step_kernel, out_shape=(jax.ShapeDtypeStruct(hidden.shape,...  27.6 us
    pallas_call x1, Pallas kernels, reduce_all(): pl.pallas_call(functools.partial(reduce_kernel, n_space, n_dp), out_shape...  18.1 us
    pallas_call x1, Pallas kernels, exchange_halo(): pl.pallas_call(functools.partial(halo_kernel, n), out_shape=jax.ShapeDtyp...  7.63 us
    unnamed x3, local copies, waits for them, and re-layouts  2.19 us
    slice x1, local copies, waits for them, and re-layouts, shards(): return (hidden_next, cell_next, total[:, :depth], total[:, depth])  1.41 us

profile of v2, /device:TPU:0, one launch (start us, length us, event | category | flops | bytes accessed | tf_op | source)
XLA Modules:
  0.0 58.2 jit_solution(7443434637504471458)
XLA Ops:
  0.6 0.0 copy-start
  0.7 0.6 %copy-done = s32[1,128]{1,0:T(1,128)S(1)} copy-done((s32[1,128]{1,0:T(1,128)S(1)}, s32[1,128]{1,0:T(1,128)}, u32[]{:S(2)}) %copy-start) | copy-done | bytes 536
  1.3 0.6 dynamic-slice_bitcast_fusion.flags
  1.9 7.6 %halo.1 = bf16[2,80,512]{2,1,0:T(8,128)(2,1)} custom-call(bf16[1,16,16,8,128]{4,3,2,1,0:T(8,128)(2,1)} %forcing.3, bf16[1,16,64,8,128]{4,3,2,1,0:T(8,128)(2,1)} %hidden.3), custom_call_target="tpu_custom_call" | custom-call | tf_op jit(solution)/shard_map/halo/pallas_call | solution.py:105
  9.5 27.6 %step.1 = (bf16[1,16,64,8,128]{4,3,2,1,0:T(8,128)(2,1)}, bf16[1,16,64,8,128]{4,3,2,1,0:T(8,128)(2,1)}, bf16[4,8,16,384]{3,2,1,0:T(8,128)(2,1)}) custom-call(s32[16]{0:T(128)} %dynamic-slice_bitcast_fusion.flags, bf16[2,80,512]{2,1,0:T(8,128)(2,1)} %halo.1, bf16[1,16,16,8,128]{4,3,2,1,0:T(8,128)(2,1)} %forcing.3, bf16[1,16,64,8,128]{4,3,2,1,0:T(8,128)(2,1)} %hidden.3, ...), custom_call_target="tpu_custom_call" | custom-call | flops 12079595520 | bytes 12582912 | tf_op jit(solution)/shard_map/step/pallas_call | solution.py:321
  37.1 18.1 %reduce.3 = f32[32,768]{1,0:T(8,128)} custom-call(bf16[4,8,16,384]{3,2,1,0:T(8,128)(2,1)} %get-tuple-element.9.sums), custom_call_target="tpu_custom_call" | custom-call | tf_op jit(solution)/shard_map/reduce/pallas_call | solution.py:443
  55.3 1.4 %slice_reduce_fusion = f32[32]{0:T(128)} fusion(f32[32,768]{1,0:T(8,128)} %reduce.3), kind=kLoop, calls=%fused_computation | loop fusion | bytes 256 | tf_op jit(solution)/shard_map/slice | solution.py:485
  56.7 1.5 %copy.12 = f32[32,720]{1,0:T(8,128)} copy(f32[32,720]{1,0:T(8,128)} %bitcast.5) | data formatting | bytes 184320
Async XLA Ops:
  0.6 0.7 %copy-start = (s32[1,128]{1,0:T(1,128)S(1)}, s32[1,128]{1,0:T(1,128)}, u32[]{:S(2)}) copy-start(s32[1,128]{1,0:T(1,128)} %param.13) | copy-start | bytes 1540

commit v3 on v2

--- a/solution.py
+++ b/solution.py
@@ -10,7 +10,7 @@
 TW = 4
 MESH = pl.DeviceIdType.MESH
 CHUNK = 16
-GROUP = 4
+GROUP = 2
 
 
 def halo_kernel(n, forcing, hidden, out, f_edge, h_edge, stage, send, landed, in_sem, send_sem, recv_sem):
@@ -165,7 +165,7 @@
     bbuf[...] = jnp.broadcast_to(gate_bias[...], (cols, gates)).T * half
     acc[...] = jnp.zeros(acc.shape, acc.dtype)
     bias_acc[...] = jnp.zeros(bias_acc.shape, bias_acc.dtype)
-    field[(bands * rows + 2) * per :, :] = jnp.zeros((padded - depth, span), field.dtype)
+    field[(bands * rows + 2) * per :, :] = jnp.zeros((per + padded - depth, span), field.dtype)
 
     lane = lax.broadcasted_iota(jnp.int32, (width, span), 1)
 
@@ -202,73 +202,111 @@
     put_row(0, edges[0].astype(jnp.float32))
     put_row(bands * rows + 1, edges[1].astype(jnp.float32))
 
+    base_tile = lax.axis_index("space") * tiles
+    gate[...] = jnp.zeros(gate.shape, gate.dtype)
+
+    def patches(line, c0=0, c1=span):
+        return field[pl.ds(pl.multiple_of(line * per, 16), padded), c0:c1]
+
+    def forward(line, slot, part):
+        c0, c1 = part * (span // 2), (part + 1) * (span // 2)
+        pre[slot, :, c0:c1] = jnp.dot(
+            wbuf[...], patches(line, c0, c1), preferred_element_type=jnp.float32
+        )
+
+    def backward(line, slot, part):
+        lines = slice(part * (padded // 2), (part + 1) * (padded // 2))
+        seen = jnp.concatenate(
+            [
+                field[pl.ds(pl.multiple_of((line + k) * per + lines.start, 16), padded // 2), :]
+                for k in range(GROUP)
+            ],
+            axis=1,
+        )
+        acc[lines, :] += lax.dot_general(
+            seen, gate[slot], (((1,), (1,)), ((), ())), preferred_element_type=jnp.float32
+        )
+
+    def stage_state(band, into, tile, c0, c1):
+        slot = lax.rem(into, 2)
+        live = jnp.where(flags[0, base_tile + band * TW + tile] >= 0, 1.0, 0.0).astype(jnp.float32)
+        lines = pl.ds((tile * hid + c0) * rows, (c1 - c0) * rows)
+        flat = ((c1 - c0) * rows, cols)
+        cs[slot, lines] = cv[band * TW + tile, c0:c1].astype(jnp.float32).reshape(flat)
+        gs[slot, lines] = gv[band * TW + tile, c0:c1].astype(jnp.float32).reshape(flat) * live
+
+    def pointwise(i, r, between):
+        slot, group = r % 2, r // GROUP
+        state = lax.rem(i, 2)
+        for number, ch in enumerate(range(0, hid, CHUNK)):
+            lines = [slice(g * hid + ch, g * hid + ch + CHUNK) for g in range(4)]
+            bias = [bbuf[lines[g], :] for g in range(4)]
+            totals = [None] * 4
+            between[number]()
+            for tile in range(TW):
+                at = pl.ds(tile * hid * rows + ch * rows + r, CHUNK, stride=rows)
+                c0, c1 = tile * cols, (tile + 1) * cols
+                t_in, t_forget, t_out, cand = [
+                    jnp.tanh(pre[slot, lines[g], c0:c1] + bias[g]) for g in range(4)
+                ]
+                in_gate = 0.5 * t_in + 0.5
+                forget = 0.5 * t_forget + 0.5
+                out_gate = 0.5 * t_out + 0.5
+                before = cs[state, at, :]
+                up = gs[state, at, :]
+                now = forget * before + in_gate * cand
+                squashed = jnp.tanh(now)
+                hs[at, :] = out_gate * squashed
+                ns[at, :] = now
+                d_cell = up * out_gate * (1.0 - squashed * squashed)
+                grads = (
+                    d_cell * cand * (1.0 - t_in * t_in),
+                    d_cell * before * (1.0 - t_forget * t_forget),
+                    up * squashed * (1.0 - t_out * t_out),
+                    d_cell * in_gate * (1.0 - cand * cand),
+                )
+                d0 = (r % GROUP) * span + c0
+                for g in range(4):
+                    gate[group % 2, lines[g], d0 : d0 + cols] = grads[g].astype(gate.dtype)
+                    totals[g] = grads[g] if totals[g] is None else totals[g] + grads[g]
+            for g in range(4):
+                bias_acc[lines[g], :] += totals[g]
+
+    load(cell, cv, c_sem, 0).wait()
+    load(grad, gv, g_sem, 0).wait()
+    for tile in range(TW):
+        stage_state(0, 0, tile, 0, hid)
+    for part in range(2):
+        forward(0, 0, part)
+    assert rows % (2 * GROUP) == 0 and GROUP == 2 and hid // CHUNK >= 4
+
     @pl.loop(0, bands)
     def _(i):
-        load(cell, cv, c_sem, i).wait()
-        load(grad, gv, g_sem, i).wait()
-
-        def patches(r):
-            return field[pl.ds(pl.multiple_of((i * rows + r) * per, 16), padded), :]
-
-        def forward(r):
-            pre[r % 2] = jnp.dot(wbuf[...], patches(r), preferred_element_type=jnp.float32)
-
-        def backward(group):
-            seen = jnp.concatenate([patches(r) for r in range(group * GROUP, (group + 1) * GROUP)], axis=1)
-            acc[...] += lax.dot_general(
-                seen, gate[group % 2], (((1,), (1,)), ((), ())), preferred_element_type=jnp.float32
-            )
-
-        def pointwise(r):
-            slot, group = r % 2, r // GROUP
-            for ch in range(0, hid, CHUNK):
-                lines = [slice(g * hid + ch, g * hid + ch + CHUNK) for g in range(4)]
-                bias = [bbuf[lines[g], :] for g in range(4)]
-                totals = [None] * 4
-                for tile in range(TW):
-                    at = pl.ds(tile * hid * rows + ch * rows + r, CHUNK, stride=rows)
-                    c0, c1 = tile * cols, (tile + 1) * cols
-                    t_in, t_forget, t_out, cand = [
-                        jnp.tanh(pre[slot, lines[g], c0:c1] + bias[g]) for g in range(4)
-                    ]
-                    in_gate = 0.5 * t_in + 0.5
-                    forget = 0.5 * t_forget + 0.5
-                    out_gate = 0.5 * t_out + 0.5
-                    before = cs[at, :]
-                    up = gs[at, :]
-                    now = forget * before + in_gate * cand
-                    squashed = jnp.tanh(now)
-                    hs[at, :] = out_gate * squashed
-                    ns[at, :] = now
-                    d_cell = up * out_gate * (1.0 - squashed * squashed)
-                    grads = (
-                        d_cell * cand * (1.0 - t_in * t_in),
-                        d_cell * before * (1.0 - t_forget * t_forget),
-                        up * squashed * (1.0 - t_out * t_out),
-                        d_cell * in_gate * (1.0 - cand * cand),
-                    )
-                    d0 = (r % GROUP) * span + c0
-                    for g in range(4):
-                        gate[group % 2, lines[g], d0 : d0 + cols] = grads[g].astype(gate.dtype)
-                        totals[g] = grads[g] if totals[g] is None else totals[g] + grads[g]
-                for g in range(4):
-                    bias_acc[lines[g], :] += totals[g]
-
-        forward(0)
+        following = jnp.minimum(i + 1, bands - 1)
+
+        @pl.when(i + 1 < bands)
+        def _():
+            load(cell, cv, c_sem, i + 1).wait()
+            load(grad, gv, g_sem, i + 1).wait()
+
+        for r in range(rows):
+            line = i * rows + r
+            earlier = jnp.maximum(i * rows + (r // GROUP - 1) * GROUP, 0)
+            share = hid * TW // rows
+            tile, c0 = r * share // hid, r * share % hid
+
+            def last(tile=tile, c0=c0):
+                stage_state(following, i + 1, tile, c0, c0 + share)
+
+            between = [
+                functools.partial(forward, line + 1, (r + 1) % 2, 0),
+                functools.partial(forward, line + 1, (r + 1) % 2, 1),
+                functools.partial(backward, earlier, (r // GROUP - 1) % 2, r % GROUP),
+                last,
+            ] + [lambda: None] * (hid // CHUNK)
+            pointwise(i, r, between)
         for tile in range(TW):
-            live = jnp.where(flags[i * TW + tile] >= 0, 1.0, 0.0).astype(jnp.float32)
-            lines = pl.ds(tile * hid * rows, hid * rows)
-            cs[lines] = cv[i * TW + tile].astype(jnp.float32).reshape(hid * rows, cols)
-            gs[lines] = gv[i * TW + tile].astype(jnp.float32).reshape(hid * rows, cols) * live
-        for r in range(rows):
-            if r + 1 < rows:
-                forward(r + 1)
-            if r % GROUP == 0 and r > 0:
-                backward(r // GROUP - 1)
-            pointwise(r)
-        backward(rows // GROUP - 1)
-        for tile in range(TW):
-            live = flags[i * TW + tile] >= 0
+            live = flags[0, base_tile + i * TW + tile] >= 0
             lines = pl.ds(tile * hid * rows, hid * rows)
             where = i * TW + tile
             keep = jnp.where(live, 1.0, 0.0).astype(jnp.float32)
@@ -282,6 +320,8 @@
         store(ho, hidden_out, ho_sem, i).start()
         store(co, cell_out, co_sem, i).start()
 
+    for part in range(2):
+        backward(bands * rows - GROUP, (rows // GROUP - 1) % 2, part)
     quarter = jnp.where(row < 3 * hid, 0.25, 1.0).astype(jnp.float32)
     bias_sum = jnp.sum(bias_acc[...], axis=1, keepdims=True) * quarter
     column = lax.broadcasted_iota(jnp.int32, (gates, padded), 1)
@@ -334,10 +374,10 @@
             pltpu.VMEM(state, jnp.bfloat16),
             pltpu.VMEM(state, jnp.bfloat16),
             pltpu.VMEM(state, jnp.bfloat16),
-            pltpu.VMEM(((bands * rows + 2) * 3 * width + padded - depth, span), jnp.bfloat16),
+            pltpu.VMEM(((bands * rows + 3) * 3 * width + padded - depth, span), jnp.bfloat16),
             pltpu.VMEM((TW * width * rows, cols), jnp.float32),
-            pltpu.VMEM(flat, jnp.float32),
-            pltpu.VMEM(flat, jnp.float32),
+            pltpu.VMEM((2,) + flat, jnp.float32),
+            pltpu.VMEM((2,) + flat, jnp.float32),
             pltpu.VMEM(flat, jnp.float32),
             pltpu.VMEM(flat, jnp.float32),
             pltpu.VMEM((gates, padded), jnp.bfloat16),
@@ -465,9 +505,7 @@
 
 
 def shards(n_space, n_dp, forcing, hidden_prev, cell_prev, hidden_grad, w_gates, gate_bias, worker):
-    tiles = forcing.shape[1]
     gates, depth = w_gates.shape
-    mine = lax.dynamic_slice_in_dim(worker[0], lax.axis_index("space") * tiles, tiles)
     halo = exchange_halo(forcing, hidden_prev, n_space)
     padded = -(-(depth + 1) // 256) * 256
     sub, ragged = divmod(gates, n_space * n_dp)
@@ -476,7 +514,7 @@
     if staged:
         sums = jax.ShapeDtypeStruct((n_dp, n_space, 2 * sub, padded // 2), jnp.bfloat16)
     hidden_next, cell_next, sums = run_step(
-        sums, mine, halo, forcing, hidden_prev, cell_prev, hidden_grad, w_gates.T, gate_bias[None, :]
+        sums, worker, halo, forcing, hidden_prev, cell_prev, hidden_grad, w_gates.T, gate_bias[None, :]
     )
     if staged:
         total = reduce_all(sums, gates)

time: 58.5 us -> 56.3 us (0.962)
  local copies, waits for them, and re-layouts: 4.18 us -> 2.95 us
  Pallas kernels: 53.4 us -> 52.5 us
    pallas_call x1, Pallas kernels: 27.6 us -> 26.7 us  [run_step(): pl.pallas_call(step_kernel, out_shape=(jax.ShapeDtypeStruct(hidden.shape,...]
    unnamed x3 -> x1, local copies, waits for them, and re-layouts: 2.19 us -> 1.54 us
where the time goes in v3:
time: 56.3 us; the launch traced here: 56.1 us
  Pallas kernels  52.5 us (93%)
  local copies, waits for them, and re-layouts  2.95 us (5%)
  between operations  0.65 us (1%)
    pallas_call x1, Pallas kernels, run_step(): pl.pallas_call(step_kernel, out_shape=(jax.ShapeDtypeStruct(hidden.shape,...  26.7 us
    pallas_call x1, Pallas kernels, reduce_all(): pl.pallas_call(functools.partial(reduce_kernel, n_space, n_dp), out_shape...  18.1 us
    pallas_call x1, Pallas kernels, exchange_halo(): pl.pallas_call(functools.partial(halo_kernel, n), out_shape=jax.ShapeDtyp...  7.65 us
    unnamed x1, local copies, waits for them, and re-layouts  1.54 us
    slice x1, local copies, waits for them, and re-layouts, shards(): return (hidden_next, cell_next, total[:, :depth], total[:, depth])  1.41 us

profile of v3, /device:TPU:0, one launch (start us, length us, event | category | flops | bytes accessed | tf_op | source)
XLA Modules:
  0.0 56.1 jit_solution(17850731563092739683)
XLA Ops:
  0.6 7.6 %halo.1 = bf16[2,80,512]{2,1,0:T(8,128)(2,1)} custom-call(bf16[1,16,16,8,128]{4,3,2,1,0:T(8,128)(2,1)} %forcing.3, bf16[1,16,64,8,128]{4,3,2,1,0:T(8,128)(2,1)} %hidden.3), custom_call_target="tpu_custom_call" | custom-call | tf_op jit(solution)/shard_map/halo/pallas_call | solution.py:105
  8.3 26.7 %step.1 = (bf16[1,16,64,8,128]{4,3,2,1,0:T(8,128)(2,1)}, bf16[1,16,64,8,128]{4,3,2,1,0:T(8,128)(2,1)}, bf16[4,8,16,384]{3,2,1,0:T(8,128)(2,1)}) custom-call(s32[1,128]{1,0:T(1,128)} %flags.1, bf16[2,80,512]{2,1,0:T(8,128)(2,1)} %halo.1, bf16[1,16,16,8,128]{4,3,2,1,0:T(8,128)(2,1)} %forcing.3, bf16[1,16,64,8,128]{4,3,2,1,0:T(8,128)(2,1)} %hidden.3, ...), custom_call_target="tpu_custom_call" | custom-call | flops 12079595520 | bytes 12582912 | tf_op jit(solution)/shard_map/step/pallas_call | solution.py:361
  35.0 18.1 %reduce.3 = f32[32,768]{1,0:T(8,128)} custom-call(bf16[4,8,16,384]{3,2,1,0:T(8,128)(2,1)} %get-tuple-element.9.sums), custom_call_target="tpu_custom_call" | custom-call | tf_op jit(solution)/shard_map/reduce/pallas_call | solution.py:483
  53.1 1.4 %slice_reduce_fusion = f32[32]{0:T(128)} fusion(f32[32,768]{1,0:T(8,128)} %reduce.3), kind=kLoop, calls=%fused_computation | loop fusion | bytes 256 | tf_op jit(solution)/shard_map/slice | solution.py:523
  54.5 1.5 %copy.12 = f32[32,720]{1,0:T(8,128)} copy(f32[32,720]{1,0:T(8,128)} %bitcast.3) | data formatting | bytes 184320
